TPU v7x, 32 devices: a whole 2x2x4 slice. The times are simulated.
32 devices in a mesh: role: 2 (over x), seq: 4 (over y, core), head: 4 (over z).
Axes of the slice: x: 2, y: 2, z: 4, core: 2. Of those that a mesh axis runs over, the one named last changes fastest.
Arguments:
- query_heads: bfloat16 [512, 16, 128], P('seq', ('role', 'head')), may hold values from -16 to 16
- key_heads: bfloat16 [512, 8, 128], P('seq', ('role', 'head')), may hold values from -16 to 16
- value_heads: bfloat16 [512, 8, 128], P('seq', ('role', 'head')), may hold values from -6 to 6
- distill_proj: bfloat16 [16, 128, 1024], P(('role', 'head')), may hold values from -6 to 6
- conv_input: bfloat16 [1024, 512], P(('role', 'head'), 'seq'), may hold values from -6 to 6
- gate_input: bfloat16 [1024, 512], P(('role', 'head'), 'seq'), may hold values from -6 to 6
- filter_taps: float32 [1024, 512], P(('role', 'head'), 'seq'), may hold values from -0.25 to 0.25
- skip_gain: float32 [1024], P(('role', 'head')), may hold values from -4 to 4
Outputs:
- grad_input: float32 [1024, 512], P(('role', 'head'), 'seq')
- filter_step: float32 [1024, 512], P(('role', 'head'), 'seq')
All inputs are finite; a program needn't handle non-finite values.
Results may differ from a plain program's by a relative error of at most 0.005.
Values may be sent and summed in bfloat16 or wider, within the bound.
A program may use at most 64 MiB of HBM per device.

v0:
```python
import math

import jax
import jax.numpy as jnp
from jax import lax
from jax.sharding import PartitionSpec as P

WINDOW = 4096


highest = lax.Precision.HIGHEST


def shifted(value, axis, steps):
    count = lax.axis_size(axis)
    leading, last = (max(0, -steps), min(count, count - steps))
    return lax.ppermute(value, axis, [(source, source + steps) for source in range(leading, last)])


def angle_table(row_ids, col_ids, length):
    product = row_ids[:, None] * col_ids[None, :] % length
    quarter = length // 4
    eighth = length // 8
    quadrant = product // quarter
    within = product % quarter
    flipped = within > eighth
    reduced = jnp.where(flipped, quarter - within, within)
    angles = reduced.astype(jnp.float32) * (2.0 * math.pi / length)
    base_cos = jnp.cos(angles)
    base_sin = jnp.sin(angles)
    first_cos = jnp.where(flipped, base_sin, base_cos)
    first_sin = jnp.where(flipped, base_cos, base_sin)
    cosine = jnp.where(
        quadrant == 0,
        first_cos,
        jnp.where(quadrant == 1, -first_sin, jnp.where(quadrant == 2, -first_cos, first_sin)),
    )
    sine_part = jnp.where(
        quadrant == 0,
        first_sin,
        jnp.where(quadrant == 1, first_cos, jnp.where(quadrant == 2, -first_sin, -first_cos)),
    )
    return (cosine, sine_part)


def spread_rows(stacked):
    pieces = stacked.shape[2]
    cosine, sine_part = angle_table(
        jnp.arange(2 * pieces, dtype=jnp.int32), jnp.arange(pieces, dtype=jnp.int32), 2 * pieces
    )
    real_part = jnp.einsum("kd,ncdr->nckr", cosine, stacked, precision=highest)
    imag_part = -jnp.einsum("kd,ncdr->nckr", sine_part, stacked, precision=highest)
    return (real_part, imag_part)


def twist(real_part, imag_part, freq_ids, time_ids, length, turning):
    cosine, sine_part = angle_table(freq_ids, time_ids, length)
    return (
        real_part * cosine - turning * imag_part * sine_part,
        imag_part * cosine + turning * real_part * sine_part,
    )


def along_block(real_part, imag_part, turning):
    length = real_part.shape[-1]
    cosine, sine_part = angle_table(
        jnp.arange(length, dtype=jnp.int32), jnp.arange(length, dtype=jnp.int32), length
    )
    out_real = jnp.einsum(
        "nckb,bj->nckj", real_part, cosine, precision=highest
    ) - turning * jnp.einsum("nckb,bj->nckj", imag_part, sine_part, precision=highest)
    out_imag = jnp.einsum(
        "nckb,bj->nckj", imag_part, cosine, precision=highest
    ) + turning * jnp.einsum("nckb,bj->nckj", real_part, sine_part, precision=highest)
    return (out_real, out_imag)


def gather_rows(real_part, imag_part, length):
    doubled = real_part.shape[2]
    cosine, sine_part = angle_table(
        jnp.arange(doubled // 2, dtype=jnp.int32), jnp.arange(doubled, dtype=jnp.int32), doubled
    )
    signal = jnp.einsum("dk,nckr->ncdr", cosine, real_part, precision=highest) - jnp.einsum(
        "dk,nckr->ncdr", sine_part, imag_part, precision=highest
    )
    return signal / length


def student(signal, gate_part, taps, target, skip_part, forward, inverse, seq_total):
    spec_real, spec_imag = forward(jnp.stack([signal, taps]))
    input_re, taps_re = (spec_real[0], spec_real[1])
    input_im, taps_im = (spec_imag[0], spec_imag[1])
    conv_re = input_re * taps_re - input_im * taps_im
    conv_im = input_re * taps_im + input_im * taps_re
    convolved = inverse(conv_re[None], conv_im[None])[0]
    output = gate_part * (convolved + skip_part[:, None] * signal)
    backed = gate_part * (output - target)
    back_real, back_imag = forward(backed[None])
    back_re, back_im = (back_real[0], back_imag[0])
    left_re = taps_re * back_re + taps_im * back_im
    left_im = taps_re * back_im - taps_im * back_re
    right_re = input_re * back_re + input_im * back_im
    right_im = input_re * back_im - input_im * back_re
    corrected = inverse(jnp.stack([left_re, right_re]), jnp.stack([left_im, right_im]))
    grad_input = skip_part[:, None] * backed + corrected[0]
    filter_step = corrected[1] * seq_total ** (-0.5)
    return (grad_input, filter_step)


def body(
    query_heads,
    key_heads,
    value_heads,
    distill_proj,
    conv_input,
    gate_input,
    filter_taps,
    skip_gain,
):
    shard_len = query_heads.shape[0]
    kv_local = key_heads.shape[1]
    per_group = query_heads.shape[1] // kv_local
    head_dim = query_heads.shape[2]
    devices = lax.axis_size("seq")
    seq_rank = lax.axis_index("seq")
    shards = min((WINDOW + shard_len - 1) // shard_len, devices - 1)
    per_step = max(1, 512 // shard_len)
    total_shards = -(-(shards + 1) // per_step) * per_step
    own_block = jnp.stack([key_heads, value_heads])
    buffer = jnp.concatenate(
        [jnp.zeros((total_shards - 1,) + own_block.shape, jnp.bfloat16), own_block[None]], axis=0
    )

    def fetch(step_id, carried):
        current, stored = carried
        current = shifted(current, "seq", 1)
        stored = lax.dynamic_update_index_in_dim(stored, current, total_shards - 1 - step_id, 0)
        return (current, stored)

    buffer = lax.fori_loop(1, shards + 1, fetch, (own_block, buffer))[1]
    key_span = per_step * shard_len
    blocks = total_shards // per_step
    keys_all = buffer[:, 0].reshape(blocks, key_span, kv_local, head_dim)
    values_all = buffer[:, 1].reshape(blocks, key_span, kv_local, head_dim)
    first_key = (seq_rank + 1 - total_shards) * shard_len
    query_pos = seq_rank * shard_len + jnp.arange(shard_len, dtype=jnp.int32)
    queries = query_heads.reshape(shard_len, kv_local, per_group, head_dim)
    score_scale = head_dim ** (-0.5)
    block_ids = jnp.arange(blocks, dtype=jnp.int32)

    def online_step(carried, element):
        row_max, row_sum, weighted = carried
        block_id, key_block, value_block = element
        scores = (
            jnp.einsum("qgae,kge->gaqk", queries, key_block, preferred_element_type=jnp.float32)
            * score_scale
        )
        key_pos = first_key + block_id * key_span + jnp.arange(key_span, dtype=jnp.int32)
        in_window = (
            (key_pos[None, :] <= query_pos[:, None])
            & (key_pos[None, :] > query_pos[:, None] - WINDOW)
            & (key_pos[None, :] >= 0)
        )
        new_max = jnp.maximum(row_max, jnp.max(jnp.where(in_window, scores, -jnp.inf), axis=-1))
        safe_max = jnp.where(new_max == -jnp.inf, 0.0, new_max)
        rescale = jnp.exp(row_max - safe_max)
        weight = jnp.where(in_window, jnp.exp(scores - safe_max[..., None]), 0.0)
        row_sum = row_sum * rescale + jnp.sum(weight, axis=-1)
        weighted = weighted * jnp.transpose(rescale, (2, 0, 1))[..., None] + jnp.einsum(
            "gaqk,kge->qgae",
            weight.astype(jnp.bfloat16),
            value_block,
            preferred_element_type=jnp.float32,
        )
        return ((new_max, row_sum, weighted), None)

    start_state = (
        jnp.full((kv_local, per_group, shard_len), -jnp.inf, jnp.float32),
        jnp.zeros((kv_local, per_group, shard_len), jnp.float32),
        jnp.zeros((shard_len, kv_local, per_group, head_dim), jnp.float32),
    )
    final_state = lax.scan(online_step, start_state, (block_ids, keys_all, values_all))[0]
    row_sum, weighted = (final_state[1], final_state[2])
    attended = (
        (weighted / jnp.transpose(row_sum, (2, 0, 1))[..., None])
        .reshape(shard_len, kv_local * per_group, head_dim)
        .astype(jnp.bfloat16)
    )
    target = lax.psum_scatter(
        jnp.einsum("the,hec->ct", attended, distill_proj, preferred_element_type=jnp.float32),
        ("role", "head"),
        scatter_dimension=0,
        tiled=True,
    )
    signal = conv_input.astype(jnp.float32)
    gate_part = gate_input.astype(jnp.float32)
    full_len = 2 * devices * shard_len
    seq_total = devices * shard_len
    freq_all = jnp.arange(2 * devices, dtype=jnp.int32)
    time_all = jnp.arange(shard_len, dtype=jnp.int32)
    part_len = shard_len // devices
    freq_mine = 2 * seq_rank + jnp.arange(2, dtype=jnp.int32)
    time_mine = seq_rank * part_len + jnp.arange(part_len, dtype=jnp.int32)

    def to_rows(stacked):
        return lax.all_to_all(stacked, "seq", split_axis=3, concat_axis=2, tiled=True)

    def to_cols(stacked):
        return lax.all_to_all(stacked, "seq", split_axis=2, concat_axis=3, tiled=True)

    def forward(stacked):
        pieces = stacked.shape[0]
        arrived = to_rows(stacked[:, :, None, :])
        real_part, imag_part = spread_rows(arrived)
        real_part, imag_part = twist(real_part, imag_part, freq_all, time_mine, full_len, -1.0)
        joined = to_cols(jnp.concatenate([real_part, imag_part], axis=0))
        return along_block(joined[:pieces], joined[pieces:], -1.0)

    def inverse(real_part, imag_part):
        pieces = real_part.shape[0]
        real_part, imag_part = along_block(real_part, imag_part, 1.0)
        real_part, imag_part = twist(real_part, imag_part, freq_mine, time_all, full_len, 1.0)
        arrived = to_rows(jnp.concatenate([real_part, imag_part], axis=0))
        rebuilt = gather_rows(arrived[:pieces], arrived[pieces:], full_len)
        return to_cols(rebuilt)[:, :, 0, :]

    grad_input, filter_step = student(
        signal, gate_part, filter_taps, target, skip_gain, forward, inverse, seq_total
    )
    return (grad_input, filter_step)


def solution(mesh):
    in_specs = (
        P("seq", ("role", "head"), None),
        P("seq", ("role", "head"), None),
        P("seq", ("role", "head"), None),
        P(("role", "head"), None, None),
        P(("role", "head"), "seq"),
        P(("role", "head"), "seq"),
        P(("role", "head"), "seq"),
        P(("role", "head")),
    )
    out_specs = (P(("role", "head"), "seq"), P(("role", "head"), "seq"))
    return jax.shard_map(body, mesh=mesh, in_specs=in_specs, out_specs=out_specs, check_vma=False)
```

profile of v0, /device:TPU:0, one launch (start us, length us, event | category | flops | bytes accessed | tf_op | source)
XLA Modules:
  0.0 157.2 jit_solution(17957275091762563368)
XLA Ops:
  7.2 0.9 copy.99
  8.3 0.8 copy.101
  9.0 4.4 %all-to-all-start = ((f32[2,128,1,128]{1,0,2,3:T(2,128)}), f32[2,128,1,128]{1,0,2,3:T(2,128)S(1)}, u32[]{:S(2)}, u32[]{:S(2)}) async-start(f32[2,128,1,128]{1,0,2,3:T(2,128)} %copy.101), calls=%async_computation | async-start | bytes 262144 | tf_op jit(solution)/shard_map/all_to_all | solution.py:206
  13.5 13.9 %while.4 = (s32[]{:T(128)}, bf16[2,128,1,128]{3,1,0,2:T(8,128)(2,1)S(1)}, bf16[4,2,128,1,128]{4,2,1,3,0:T(8,128)(2,1)S(1)}, s32[]{:T(128)}, s32[]{:T(128)}, /*index=5*/s32[]{:T(128)}, s32[]{:T(128)}) while((s32[]{:T(128)}, bf16[2,128,1,128]{3,1,0,2:T(8,128)(2,1)S(1)}, bf16[4,2,128,1,128]{4,2,1,3,0:T(8,128)(2,1)S(1)}, s32[]{:T(128)}, ...), condition=%wide.region_1.2_spmd, body=%wide.region_0.1_spmd.sunk | while | flops 6 | bytes 524455 | solution.py:140
  13.5 2.4 %collective-permute-start = (bf16[2,128,1,128]{3,1,0,2:T(8,128)(2,1)S(1)}, bf16[2,128,1,128]{3,1,0,2:T(8,128)(2,1)S(1)}, u32[]{:S(2)}, u32[]{:S(2)}) collective-permute-start(bf16[2,128,1,128]{3,1,0,2:T(8,128)(2,1)S(1)} %get-tuple-element.180), channel_id=1, source_target_pairs={{0,4},{4,8},{8,12},{1,5},{5,9},{9,13},{2,6},{6,10},{10,14},{3,7},{... | collective-permute-start | bytes 196616 | tf_op jit(solution)/shard_map/while/body/eval_jaxpr/ppermute | solution.py:17
  15.9 0.9 collective-permute-done
  16.8 4.0 %collective-permute-start = (bf16[2,128,1,128]{3,1,0,2:T(8,128)(2,1)S(1)}, bf16[2,128,1,128]{3,1,0,2:T(8,128)(2,1)S(1)}, u32[]{:S(2)}, u32[]{:S(2)}) collective-permute-start(bf16[2,128,1,128]{3,1,0,2:T(8,128)(2,1)S(1)} %get-tuple-element.180), channel_id=1, source_target_pairs={{0,4},{4,8},{8,12},{1,5},{5,9},{9,13},{2,6},{6,10},{10,14},{3,7},{... | collective-permute-start | bytes 196616 | tf_op jit(solution)/shard_map/while/body/eval_jaxpr/ppermute | solution.py:17
  20.9 0.9 collective-permute-done
  21.8 4.7 %collective-permute-start = (bf16[2,128,1,128]{3,1,0,2:T(8,128)(2,1)S(1)}, bf16[2,128,1,128]{3,1,0,2:T(8,128)(2,1)S(1)}, u32[]{:S(2)}, u32[]{:S(2)}) collective-permute-start(bf16[2,128,1,128]{3,1,0,2:T(8,128)(2,1)S(1)} %get-tuple-element.180), channel_id=1, source_target_pairs={{0,4},{4,8},{8,12},{1,5},{5,9},{9,13},{2,6},{6,10},{10,14},{3,7},{... | collective-permute-start | bytes 196616 | tf_op jit(solution)/shard_map/while/body/eval_jaxpr/ppermute | solution.py:17
  26.5 0.9 collective-permute-done
  27.4 0.2 and_and_fusion
  27.7 0.6 copy-done.1
  28.3 0.3 select_reduce_fusion
  28.5 0.2 select_select_fusion.18
  28.7 0.1 fusion.15
  28.9 0.5 convolution_bitcast_fusion.1
  29.4 0.6 multiply_subtract_fusion.1
  30.0 0.9 copy.105
  30.9 6.3 %all-to-all-start.1 = ((f32[4,128,8,32]{1,3,0,2:T(8,128)}), f32[4,128,8,32]{1,3,0,2:T(8,128)S(1)}, u32[]{:S(2)}, u32[]{:S(2)}) async-start(f32[4,128,8,32]{1,3,0,2:T(8,128)} %copy.105), calls=%async_computation.1 | async-start | bytes 1048576 | tf_op jit(solution)/shard_map/all_to_all | solution.py:209
  37.2 1.3 convolution_bitcast_fusion
  38.6 0.1 select_select_fusion.28
  38.7 7.4 %all-to-all-done.1 = f32[4,128,8,32]{1,3,0,2:T(8,128)S(1)} async-done(((f32[4,128,8,32]{1,3,0,2:T(8,128)}), f32[4,128,8,32]{1,3,0,2:T(8,128)S(1)}, u32[]{:S(2)}, u32[]{:S(2)}) %all-to-all-start.1) | async-done | bytes 524320 | tf_op jit(solution)/shard_map/all_to_all | solution.py:209
  46.2 0.8 fusion.56
  47.0 0.8 fusion.58
  47.9 0.8 fusion.1
  48.7 0.8 fusion.2
  49.6 0.6 fusion.28
  50.2 0.6 fusion.32
  50.9 0.6 convolution_add_fusion.2
  51.5 0.6 subtract_bitcast_fusion
  52.2 0.2 copy.113
  52.4 8.4 %all_to_all.99 = f32[2,128,2,128]{1,2,0,3:T(2,128)S(1)} all-to-all(f32[2,128,2,128]{1,2,0,3:T(2,128)S(1)} %copy.113), channel_id=1, replica_groups=mesh['role'=2,'seq'=4,'head'=4] {'seq'}, dimensions={3} | all-to-all | bytes 524288 | tf_op jit(solution)/shard_map/all_to_all | solution.py:206
  60.8 0.1 copy.115
  60.9 0.1 copy.116
  61.0 0.3 fusion.102
  61.4 0.3 fusion.14
  61.7 0.6 copy.117
  62.3 3.4 %all-to-all-start.3 = ((f32[1,128,4,32]{1,3,0,2:T(8,128)}), f32[1,128,4,32]{1,3,0,2:T(8,128)S(1)}, u32[]{:S(2)}, u32[]{:S(2)}) async-start(f32[1,128,4,32]{1,3,0,2:T(8,128)} %copy.117), calls=%async_computation.3 | async-start | bytes 131072 | tf_op jit(solution)/shard_map/all_to_all | solution.py:209
  65.8 0.1 copy.98
  65.9 3.9 %all-to-all-done.3 = f32[1,128,4,32]{1,3,0,2:T(8,128)S(1)} async-done(((f32[1,128,4,32]{1,3,0,2:T(8,128)}), f32[1,128,4,32]{1,3,0,2:T(8,128)S(1)}, u32[]{:S(2)}, u32[]{:S(2)}) %all-to-all-start.3) | async-done | bytes 65568 | tf_op jit(solution)/shard_map/all_to_all | solution.py:209
  69.8 36.4 %reduce-scatter.2.cloned.1.call-done = f32[128,128]{0,1:T(8,128)} async-done(((f32[1024,128]{0,1:T(8,128)}), f32[128,128]{0,1:T(8,128)}) %reduce-scatter.2.cloned.1.call-update) | async-done | bytes 65552 | tf_op jit(solution)/shard_map/reduce_scatter | solution.py:189
  106.2 0.9 convert_multiply_fusion.1
  107.1 6.7 %all_to_all.100 = f32[1,128,1,128]{1,2,0,3:T(1,128)S(1)} all-to-all(f32[1,128,1,128]{1,2,0,3:T(1,128)S(1)} %bitcast.247), channel_id=1, replica_groups=mesh['role'=2,'seq'=4,'head'=4] {'seq'}, dimensions={3} | all-to-all | bytes 131072 | tf_op jit(solution)/shard_map/all_to_all | solution.py:206
  113.8 0.4 convolution_bitcast_fusion.2
  114.2 0.4 multiply_subtract_fusion.4
  114.7 8.4 %all_to_all.101 = f32[2,128,8,32]{1,3,0,2:T(8,128)S(1)} all-to-all(f32[2,128,8,32]{1,3,0,2:T(8,128)S(1)} %copy.126), channel_id=1, replica_groups=mesh['role'=2,'seq'=4,'head'=4] {'seq'}, dimensions={2} | all-to-all | bytes 524288 | tf_op jit(solution)/shard_map/all_to_all | solution.py:209
  123.2 0.6 convolution_multiply_fusion.3
  123.8 0.6 convolution_multiply_fusion.4
  124.5 0.7 fusion.5
  125.2 0.7 multiply_subtract_fusion.3
  125.8 0.7 fusion.27
  126.6 0.7 fusion.26
  127.3 0.7 convolution_subtract_fusion
  128.0 0.8 multiply_subtract_fusion
  128.8 0.3 copy.134
  129.2 11.2 %all_to_all.102 = f32[4,128,2,128]{1,2,0,3:T(2,128)S(1)} all-to-all(f32[4,128,2,128]{1,2,0,3:T(2,128)S(1)} %copy.134), channel_id=1, replica_groups=mesh['role'=2,'seq'=4,'head'=4] {'seq'}, dimensions={3} | all-to-all | bytes 1048576 | tf_op jit(solution)/shard_map/all_to_all | solution.py:206
  140.4 0.1 copy.135
  140.6 0.2 copy.136
  140.8 0.4 fusion.95
  141.2 0.2 copy.137
  141.4 0.4 fusion.8
  141.8 7.0 %all_to_all.103 = f32[2,128,4,32]{1,3,0,2:T(8,128)S(1)} all-to-all(f32[2,128,4,32]{1,3,0,2:T(8,128)S(1)} %copy.138), channel_id=1, replica_groups=mesh['role'=2,'seq'=4,'head'=4] {'seq'}, dimensions={2} | all-to-all | bytes 262144 | tf_op jit(solution)/shard_map/all_to_all | solution.py:209
  148.9 0.7 copy.140
  149.6 0.7 copy.141
  (57 shorter events, 0.8 us)
Async XLA Ops:
  7.2 30.0 %copy-start = (bf16[2,128,1024]{2,1,0:T(8,128)(2,1)S(1)}, bf16[2,128,1024]{2,1,0:T(8,128)(2,1)}, u32[]{:S(2)}) copy-start(bf16[2,128,1024]{2,1,0:T(8,128)(2,1)} %param.13) | copy-start | bytes 1572868
  7.2 1.0 copy-start.2
  9.0 4.4 %copy-start.4 = (bf16[128,1,128]{2,0,1:T(8,128)(2,1)S(1)}, bf16[128,1,128]{2,0,1:T(8,128)(2,1)}, u32[]{:S(2)}) copy-start(bf16[128,1,128]{2,0,1:T(8,128)(2,1)} %param.12) | copy-start | bytes 98308
  9.0 4.4 %copy-start.5 = (bf16[128,1,128]{2,0,1:T(8,128)(2,1)S(1)}, bf16[128,1,128]{2,0,1:T(8,128)(2,1)}, u32[]{:S(2)}) copy-start(bf16[128,1,128]{2,0,1:T(8,128)(2,1)} %param.11) | copy-start | bytes 98308
  9.0 19.8 %all-to-all-start = ((f32[2,128,1,128]{1,0,2,3:T(2,128)}), f32[2,128,1,128]{1,0,2,3:T(2,128)S(1)}, u32[]{:S(2)}, u32[]{:S(2)}) async-start(f32[2,128,1,128]{1,0,2,3:T(2,128)} %copy.101), calls=%async_computation | async-start | bytes 262144 | tf_op jit(solution)/shard_map/all_to_all | solution.py:206
  13.5 3.3 %collective-permute-start = (bf16[2,128,1,128]{3,1,0,2:T(8,128)(2,1)S(1)}, bf16[2,128,1,128]{3,1,0,2:T(8,128)(2,1)S(1)}, u32[]{:S(2)}, u32[]{:S(2)}) collective-permute-start(bf16[2,128,1,128]{3,1,0,2:T(8,128)(2,1)S(1)} %get-tuple-element.180), channel_id=1, source_target_pairs={{0,4},{4,8},{8,12},{1,5},{5,9},{9,13},{2,6},{6,10},{10,14},{3,7},{... | collective-permute-start | bytes 196616 | tf_op jit(solution)/shard_map/while/body/eval_jaxpr/ppermute | solution.py:17
  16.8 4.9 %collective-permute-start = (bf16[2,128,1,128]{3,1,0,2:T(8,128)(2,1)S(1)}, bf16[2,128,1,128]{3,1,0,2:T(8,128)(2,1)S(1)}, u32[]{:S(2)}, u32[]{:S(2)}) collective-permute-start(bf16[2,128,1,128]{3,1,0,2:T(8,128)(2,1)S(1)} %get-tuple-element.180), channel_id=1, source_target_pairs={{0,4},{4,8},{8,12},{1,5},{5,9},{9,13},{2,6},{6,10},{10,14},{3,7},{... | collective-permute-start | bytes 196616 | tf_op jit(solution)/shard_map/while/body/eval_jaxpr/ppermute | solution.py:17
  21.8 5.6 %collective-permute-start = (bf16[2,128,1,128]{3,1,0,2:T(8,128)(2,1)S(1)}, bf16[2,128,1,128]{3,1,0,2:T(8,128)(2,1)S(1)}, u32[]{:S(2)}, u32[]{:S(2)}) collective-permute-start(bf16[2,128,1,128]{3,1,0,2:T(8,128)(2,1)S(1)} %get-tuple-element.180), channel_id=1, source_target_pairs={{0,4},{4,8},{8,12},{1,5},{5,9},{9,13},{2,6},{6,10},{10,14},{3,7},{... | collective-permute-start | bytes 196616 | tf_op jit(solution)/shard_map/while/body/eval_jaxpr/ppermute | solution.py:17
  27.4 0.8 copy-start.1
  30.9 15.2 %all-to-all-start.1 = ((f32[4,128,8,32]{1,3,0,2:T(8,128)}), f32[4,128,8,32]{1,3,0,2:T(8,128)S(1)}, u32[]{:S(2)}, u32[]{:S(2)}) async-start(f32[4,128,8,32]{1,3,0,2:T(8,128)} %copy.105), calls=%async_computation.1 | async-start | bytes 1048576 | tf_op jit(solution)/shard_map/all_to_all | solution.py:209
  37.2 69.0 %reduce-scatter.2.cloned.1.call-start = ((), (), s32[]{:S(2)}) async-start(), calls=%async_computation.9 | async-start | bytes 589824 | tf_op jit(solution)/shard_map/reduce_scatter | solution.py:189
  62.3 3.4 %copy-start.3 = (bf16[128,128]{1,0:T(8,128)(2,1)S(1)}, bf16[128,128]{1,0:T(8,128)(2,1)}, u32[]{:S(2)}) copy-start(bf16[128,128]{1,0:T(8,128)(2,1)} %param.15) | copy-start | bytes 98308
  62.3 7.5 %all-to-all-start.3 = ((f32[1,128,4,32]{1,3,0,2:T(8,128)}), f32[1,128,4,32]{1,3,0,2:T(8,128)S(1)}, u32[]{:S(2)}, u32[]{:S(2)}) async-start(f32[1,128,4,32]{1,3,0,2:T(8,128)} %copy.117), calls=%async_computation.3 | async-start | bytes 131072 | tf_op jit(solution)/shard_map/all_to_all | solution.py:209
  65.8 40.5 %copy-start.6 = (f32[128]{0:T(128)S(1)}, f32[128]{0:T(128)}, u32[]{:S(2)}) copy-start(f32[128]{0:T(128)} %param.17) | copy-start | bytes 1540
Sparse Core Ops, SparseCore 0:
  41.4 64.7 reduce-scatter.1
where the time goes:
time: 158 us; the launch traced here: 157 us
  waiting for transfers between devices  50.3 us (32%)
  blocking collectives  41.8 us (26%)
  starting transfers between devices  25.2 us (16%)
  matrix products  16.2 us (10%)
  between operations  14.6 us (9%)
  local copies, waits for them, and re-layouts  7.2 us (5%)
  other arithmetic  1.72 us (1%)
    reduce_scatter x1, waiting for transfers between devices, body(): lax.psum_scatter(jnp.einsum('the,hec->ct', attended, distill_proj, prefer...  36.4 us
    all_to_all x3, blocking collectives, to_rows(): lax.all_to_all(stacked, 'seq', split_axis=3, concat_axis=2, tiled=True)  26.4 us
    all_to_all x2, blocking collectives, to_cols(): lax.all_to_all(stacked, 'seq', split_axis=2, concat_axis=3, tiled=True)  15.4 us
    all_to_all x2, waiting for transfers between devices, to_cols(): lax.all_to_all(stacked, 'seq', split_axis=2, concat_axis=3, tiled=True)  11.3 us
    ppermute x3, starting transfers between devices, shifted(): lax.ppermute(value, axis, [(source, source + steps) for source in range(l...  11.1 us
    all_to_all x2, starting transfers between devices, to_cols(): lax.all_to_all(stacked, 'seq', split_axis=2, concat_axis=3, tiled=True)  9.72 us
    all_to_all x1, starting transfers between devices, to_rows(): lax.all_to_all(stacked, 'seq', split_axis=3, concat_axis=2, tiled=True)  4.37 us
    unnamed x19, local copies, waits for them, and re-layouts  3.24 us
  transfers between devices with their start and end apart: 7, of which 6 were waited for; matrix products, arithmetic and copies ran while one was open for 6% of the time, Pallas kernels for 0%

commit v1 on v0

--- a/solution.py
+++ b/solution.py
@@ -1,13 +1,17 @@
+import functools
 import math
 
 import jax
 import jax.numpy as jnp
+import ml_dtypes
+import numpy as np
 from jax import lax
+from jax.experimental import pallas as pl
+from jax.experimental.pallas import tpu as pltpu
 from jax.sharding import PartitionSpec as P
 
 WINDOW = 4096
-
-
+MESH = pl.DeviceIdType.MESH
 highest = lax.Precision.HIGHEST
 
 
@@ -230,6 +234,304 @@
     return (grad_input, filter_step)
 
 
+def half_step_table(length):
+    product = np.arange(length)[:, None] * (2 * np.arange(length)[None, :] + 1) % (4 * length)
+    angle = product * (math.pi / (2 * length))
+    whole = np.concatenate([np.cos(angle), np.sin(angle)], axis=1)
+    upper = whole.astype(ml_dtypes.bfloat16)
+    lower = (whole - upper.astype(np.float64)).astype(ml_dtypes.bfloat16)
+    return np.stack([upper, lower])
+
+
+def fits_fused(query_heads, key_heads, value_heads, distill_proj, conv_input, gate_input, filter_taps, skip_gain):
+    seq_total = lax.axis_size("seq") * query_heads.shape[0]
+    groups = lax.axis_size("role") * lax.axis_size("head")
+    chan_local = conv_input.shape[0]
+    return (
+        seq_total <= min(WINDOW, 1024)
+        and query_heads.shape[0] % 128 == 0
+        and key_heads.shape[1] == 1
+        and key_heads.shape[2] % 128 == 0
+        and chan_local % 128 == 0
+        and chan_local * groups == distill_proj.shape[2]
+    )
+
+
+def dot_nt(left, right):
+    return lax.dot_general(left, right, (((1,), (1,)), ((), ())), preferred_element_type=jnp.float32)
+
+
+def forward(rows, table_buf, where):
+    upper = jnp.dot(rows, table_buf[0, where, :], preferred_element_type=jnp.float32)
+    return upper + jnp.dot(rows, table_buf[1, where, :], preferred_element_type=jnp.float32)
+
+
+def inverse(spec, turned_buf):
+    upper = spec.astype(jnp.bfloat16)
+    lower = (spec - upper.astype(jnp.float32)).astype(jnp.bfloat16)
+    both = jnp.concatenate([upper, lower], axis=0)
+    first = jnp.dot(both, turned_buf[0], preferred_element_type=jnp.float32)
+    second = jnp.dot(upper, turned_buf[1], preferred_element_type=jnp.float32)
+    return first[: spec.shape[0]] + (first[spec.shape[0]:] + second)
+
+
+def fused_kernel(
+    seq_n, role_n, head_n, heads,
+    query_hbm, key_hbm, value_hbm, proj_hbm, signal_hbm, gate_hbm, taps_hbm, skip_hbm, table_hbm, turned_hbm,
+    grad_ref, step_ref,
+    query_buf, key_buf, value_buf, proj_buf, gate_buf, taps_buf, skip_buf, table_buf, turned_buf,
+    pair_buf, spec_buf, out_buf, part_send, part_recv, back_buf,
+    local_sem, gather_send, gather_recv, part_send_sem, part_recv_sem, back_send, back_recv,
+):
+    group_n = role_n * head_n
+    mine = lax.axis_index("seq")
+    group = lax.axis_index("role") * head_n + lax.axis_index("head")
+    span = key_hbm.shape[0]
+    chans = gate_buf.shape[0]
+    seq_total = seq_n * span
+    head_dim = key_hbm.shape[1]
+    here = pl.ds(pl.multiple_of(mine * span, span), span)
+
+    def place(rank):
+        return pl.ds(pl.multiple_of(rank * span, span), span)
+
+    def seq_peer(step):
+        return lax.rem(mine + step, seq_n)
+
+    def seq_from(step):
+        return lax.rem(mine + seq_n - step, seq_n)
+
+    def group_peer(step):
+        other = lax.rem(group + step, group_n)
+        return other, {"role": other // head_n, "head": lax.rem(other, head_n)}
+
+    def group_from(step):
+        return lax.rem(group + group_n - step, group_n)
+
+    signal_rows, taps_rows = pl.ds(0, chans), pl.ds(chans, chans)
+    locals_ = [
+        pltpu.make_async_copy(source, target, local_sem.at[index])
+        for index, (source, target) in enumerate([
+            (taps_hbm, taps_buf),
+            (query_hbm, query_buf),
+            (key_hbm, key_buf.at[here]),
+            (value_hbm, value_buf.at[here]),
+            (signal_hbm, pair_buf.at[signal_rows, here]),
+            (proj_hbm, proj_buf),
+            (gate_hbm, gate_buf),
+            (skip_hbm, skip_buf),
+            (table_hbm, table_buf),
+            (turned_hbm.at[:, :, here], turned_buf),
+        ])
+    ]
+    for copy in locals_:
+        copy.start()
+    taps_copy, query_copy, key_copy, value_copy, signal_copy, proj_copy, gate_copy, skip_copy, table_copy, turned_copy = locals_
+
+    barrier = pltpu.get_barrier_semaphore()
+    for step in range(1, seq_n):
+        pl.semaphore_signal(barrier, inc=1, device_id={"seq": seq_peer(step)}, device_id_type=MESH)
+    for step in range(1, group_n):
+        pl.semaphore_signal(barrier, inc=1, device_id=group_peer(step)[1], device_id_type=MESH)
+    taps_copy.wait()
+    pair_buf[taps_rows, here] = taps_buf[...].astype(jnp.bfloat16)
+    rows = query_buf.shape[0]
+    row_id = lax.broadcasted_iota(jnp.int32, (rows, rows), 0)
+    col_id = lax.broadcasted_iota(jnp.int32, (rows, rows), 1)
+    wanted = (row_id % span) * heads + row_id // span
+    order = jnp.where(col_id == wanted, 1.0, 0.0).astype(jnp.bfloat16)
+    query_copy.wait()
+    queries = jnp.dot(order, query_buf[...], preferred_element_type=jnp.float32).astype(jnp.bfloat16)
+    pl.semaphore_wait(barrier, seq_n + group_n - 2)
+
+    def gather(kind, step, source, target):
+        return pltpu.make_async_remote_copy(
+            src_ref=source,
+            dst_ref=target,
+            send_sem=gather_send.at[kind, step],
+            recv_sem=gather_recv.at[kind, step],
+            device_id={"seq": seq_peer(step)},
+            device_id_type=MESH,
+        )
+
+    far_first = sorted(range(1, seq_n), key=lambda step: abs(2 * step - seq_n))
+    sends = []
+    for kind, source, target in (
+        (0, key_hbm, key_buf.at[here]),
+        (1, value_hbm, value_buf.at[here]),
+        (2, signal_hbm, pair_buf.at[signal_rows, here]),
+        (3, pair_buf.at[taps_rows, here], pair_buf.at[taps_rows, here]),
+    ):
+        for step in far_first:
+            copy = gather(kind, step, source, target)
+            copy.start()
+            sends.append(copy)
+
+    key_copy.wait()
+    value_copy.wait()
+    for step in range(1, seq_n):
+        gather(0, step, key_hbm, key_buf.at[place(seq_from(step))]).wait_recv()
+    scores = dot_nt(queries, key_buf[...]) * (head_dim ** -0.5)
+    query_pos = mine * span + lax.broadcasted_iota(jnp.int32, scores.shape, 0) % span
+    key_pos = lax.broadcasted_iota(jnp.int32, scores.shape, 1)
+    live = key_pos <= query_pos
+    row_max = jnp.max(jnp.where(live, scores, -jnp.inf), axis=1, keepdims=True)
+    weight = jnp.where(live, jnp.exp(scores - row_max), 0.0)
+    row_sum = jnp.sum(weight, axis=1, keepdims=True)
+    for step in range(1, seq_n):
+        gather(1, step, value_hbm, value_buf.at[place(seq_from(step))]).wait_recv()
+    weighted = jnp.dot(weight.astype(jnp.bfloat16), value_buf[...], preferred_element_type=jnp.float32)
+    attended = (weighted / row_sum).astype(jnp.bfloat16)
+
+    proj_copy.wait()
+    partial = jnp.dot(attended[:span], proj_buf[0], preferred_element_type=jnp.float32)
+    for head in range(1, heads):
+        partial = partial + jnp.dot(
+            attended[head * span:(head + 1) * span], proj_buf[head], preferred_element_type=jnp.float32
+        )
+    for block in range(group_n):
+        part_send[block] = partial[:, block * chans:(block + 1) * chans].astype(jnp.bfloat16)
+
+    def part_copy(step, slot):
+        other, device = group_peer(step)
+        return pltpu.make_async_remote_copy(
+            src_ref=part_send.at[other],
+            dst_ref=part_recv.at[slot],
+            send_sem=part_send_sem.at[step],
+            recv_sem=part_recv_sem.at[step],
+            device_id=device,
+            device_id_type=MESH,
+        )
+
+    for step in range(1, group_n):
+        copy = part_copy(step, step)
+        copy.start()
+        sends.append(copy)
+
+    signal_copy.wait()
+    for step in range(1, seq_n):
+        gather(2, step, signal_hbm, pair_buf.at[signal_rows, place(seq_from(step))]).wait_recv()
+        gather(3, step, pair_buf.at[taps_rows, here], pair_buf.at[taps_rows, place(seq_from(step))]).wait_recv()
+    table_copy.wait()
+    turned_copy.wait()
+    gate_copy.wait()
+    skip_copy.wait()
+    spec_buf[...] = forward(pair_buf[...], table_buf, slice(None))
+    low, high = pl.ds(0, seq_total), pl.ds(seq_total, seq_total)
+    input_c, input_s = spec_buf[signal_rows, low], spec_buf[signal_rows, high]
+    taps_c, taps_s = spec_buf[taps_rows, low], spec_buf[taps_rows, high]
+    conv_spec = jnp.concatenate(
+        [input_c * taps_c - input_s * taps_s, input_c * taps_s + input_s * taps_c], axis=1
+    )
+    conv = inverse(conv_spec, turned_buf) * (1.0 / seq_total)
+    skip = jnp.transpose(jnp.broadcast_to(skip_buf[...], (span, chans)))
+    gate = gate_buf[...].astype(jnp.float32)
+    out_buf[...] = gate * (conv + skip * pair_buf[signal_rows, here].astype(jnp.float32))
+
+    target = part_send[group].astype(jnp.float32)
+    for step in range(1, group_n):
+        part_copy(step, step).wait_recv()
+        target = target + part_recv[step].astype(jnp.float32)
+    back = gate * (out_buf[...] - jnp.transpose(target))
+    back_buf[:, here] = back.astype(jnp.bfloat16)
+
+    def back_copy(step, owner):
+        where = place(owner)
+        return pltpu.make_async_remote_copy(
+            src_ref=back_buf.at[:, here],
+            dst_ref=back_buf.at[:, where],
+            send_sem=back_send.at[step],
+            recv_sem=back_recv.at[owner],
+            device_id={"seq": seq_peer(step)},
+            device_id_type=MESH,
+        )
+
+    for step in far_first:
+        copy = back_copy(step, mine)
+        copy.start()
+        sends.append(copy)
+    width = 2 if seq_n % 2 == 0 else 1
+    back_spec = 0.0
+    for step in range(seq_n // width):
+        first = lax.rem(mine // width + step, seq_n // width) * width
+        for owner in ([lax.rem(mine + 1, 2) + first] if step == 0 and width == 2 else []) + (
+            [first + inner for inner in range(width)] if step else []
+        ):
+            back_copy(1, owner).wait_recv()
+        where = pl.ds(pl.multiple_of(first * span, width * span), width * span)
+        back_spec = back_spec + forward(back_buf[:, where], table_buf, where)
+    back_c, back_s = back_spec[:, :seq_total], back_spec[:, seq_total:]
+
+    def correlation(rows):
+        first_c, first_s = spec_buf[rows, low], spec_buf[rows, high]
+        return jnp.concatenate([first_c * back_c + first_s * back_s, first_c * back_s - first_s * back_c], axis=1)
+
+    lags = inverse(jnp.concatenate([correlation(taps_rows), correlation(signal_rows)], axis=0), turned_buf)
+    grad_ref[...] = skip * back + lags[:chans] * (1.0 / seq_total)
+    step_ref[...] = lags[chans:] * (seq_total ** -1.5)
+    for copy in sends:
+        copy.wait_send()
+
+
+def fused_body(query_heads, key_heads, value_heads, distill_proj, conv_input, gate_input, filter_taps, skip_gain):
+    span, heads, head_dim = query_heads.shape
+    seq_n, role_n, head_n = (lax.axis_size(axis) for axis in ("seq", "role", "head"))
+    group_n = role_n * head_n
+    seq_total = seq_n * span
+    chans = conv_input.shape[0]
+    table_terms = half_step_table(seq_total)
+    table = jnp.asarray(table_terms)
+    turned = jnp.asarray(np.ascontiguousarray(np.swapaxes(table_terms, 1, 2)))
+    in_hbm = pl.BlockSpec(memory_space=pltpu.HBM)
+    vmem = pl.BlockSpec(memory_space=pltpu.VMEM)
+    bf16, f32 = jnp.bfloat16, jnp.float32
+    dma = pltpu.SemaphoreType.DMA
+    return pl.pallas_call(
+        functools.partial(fused_kernel, seq_n, role_n, head_n, heads),
+        out_shape=[jax.ShapeDtypeStruct((chans, span), f32)] * 2,
+        in_specs=[in_hbm] * 10,
+        out_specs=[vmem, vmem],
+        scratch_shapes=[
+            pltpu.VMEM((span * heads, head_dim), bf16),
+            pltpu.VMEM((seq_total, head_dim), bf16),
+            pltpu.VMEM((seq_total, head_dim), bf16),
+            pltpu.VMEM(distill_proj.shape, bf16),
+            pltpu.VMEM((chans, span), bf16),
+            pltpu.VMEM((chans, span), f32),
+            pltpu.VMEM((1, chans), f32),
+            pltpu.VMEM(table.shape, bf16),
+            pltpu.VMEM((2, 2 * seq_total, span), bf16),
+            pltpu.VMEM((2 * chans, seq_total), bf16),
+            pltpu.VMEM((2 * chans, 2 * seq_total), f32),
+            pltpu.VMEM((chans, span), f32),
+            pltpu.VMEM((group_n, span, chans), bf16),
+            pltpu.VMEM((group_n, span, chans), bf16),
+            pltpu.VMEM((chans, seq_total), bf16),
+            dma((10,)),
+            dma((4, seq_n)),
+            dma((4, seq_n)),
+            dma((group_n,)),
+            dma((group_n,)),
+            dma((seq_n,)),
+            dma((seq_n,)),
+        ],
+        compiler_params=pltpu.CompilerParams(
+            collective_id=0, has_side_effects=True, vmem_limit_bytes=63 * 1024 * 1024
+        ),
+    )(
+        query_heads.reshape(span * heads, head_dim),
+        key_heads.reshape(span, head_dim),
+        value_heads.reshape(span, head_dim),
+        distill_proj,
+        conv_input,
+        gate_input,
+        filter_taps,
+        skip_gain.reshape(1, chans),
+        table,
+        turned,
+    )
+
+
 def solution(mesh):
     in_specs = (
         P("seq", ("role", "head"), None),
@@ -242,4 +544,7 @@
         P(("role", "head")),
     )
     out_specs = (P(("role", "head"), "seq"), P(("role", "head"), "seq"))
-    return jax.shard_map(body, mesh=mesh, in_specs=in_specs, out_specs=out_specs, check_vma=False)
+    def chosen(*arrays):
+        return fused_body(*arrays) if fits_fused(*arrays) else body(*arrays)
+
+    return jax.shard_map(chosen, mesh=mesh, in_specs=in_specs, out_specs=out_specs, check_vma=False)

time: 158 us -> 27.7 us (0.18)
  waiting for transfers between devices: 50.3 us -> 0 us
  blocking collectives: 41.8 us -> 0 us
  starting transfers between devices: 25.2 us -> 0 us
  Pallas kernels: 0 us -> 23.9 us
  matrix products: 16.2 us -> 0 us
  between operations: 14.6 us -> 0.64 us
  local copies, waits for them, and re-layouts: 7.2 us -> 2.95 us
  other arithmetic: 1.72 us -> 0 us
    all_to_all x5 -> x0, blocking collectives: 41.8 us -> none  [the longest x3 26.4 us: to_rows(): lax.all_to_all(stacked, 'seq', split_axis=3, concat_axis=2, tiled=True)]
    reduce_scatter x1 -> x0, waiting for transfers between devices: 36.4 us -> none  [body(): lax.psum_scatter(jnp.einsum('the,hec->ct', attended, distill_proj, prefer...]
    pallas_call x0 -> x1, Pallas kernels: none -> 23.9 us  [fused_body(): pl.pallas_call(functools.partial(fused_kernel, seq_n, role_n, head_n, hea...]
    dot_general x26 -> x0, matrix products: 16.2 us -> none  [the longest x4 2.86 us: along_block(): jnp.einsum('nckb,bj->nckj', real_part, sine_part, precision=highest)]
    all_to_all x3 -> x0, starting transfers between devices: 14.1 us -> none  [the longest x2 9.72 us: to_cols(): lax.all_to_all(stacked, 'seq', split_axis=2, concat_axis=3, tiled=True)]
    all_to_all x3 -> x0, waiting for transfers between devices: 11.3 us -> none  [the longest x2 11.3 us: to_cols(): lax.all_to_all(stacked, 'seq', split_axis=2, concat_axis=3, tiled=True)]
    ppermute x3 -> x0, starting transfers between devices: 11.1 us -> none  [shifted(): lax.ppermute(value, axis, [(source, source + steps) for source in range(l...]
    ppermute x3 -> x0, waiting for transfers between devices: 2.62 us -> none  [shifted(): lax.ppermute(value, axis, [(source, source + steps) for source in range(l...]
  transfers between devices with their start and end apart: 7 -> 0, of which waited for: 6 -> 0; matrix products, arithmetic and copies ran while one was open for 6% -> 0% of each run, Pallas kernels for 0% -> 0%
where the time goes in v1:
time: 27.7 us; the launch traced here: 27.4 us
  Pallas kernels  23.9 us (86%)
  local copies, waits for them, and re-layouts  2.95 us (11%)
  between operations  0.64 us (2%)
    pallas_call x1, Pallas kernels, fused_body(): pl.pallas_call(functools.partial(fused_kernel, seq_n, role_n, head_n, hea...  23.9 us
    unnamed x2, local copies, waits for them, and re-layouts  2.95 us

profile of v1, /device:TPU:0, one launch (start us, length us, event | category | flops | bytes accessed | tf_op | source)
XLA Modules:
  0.0 27.4 jit_solution(9564789072779747490)
XLA Ops:
  0.6 23.9 %shard_map.113 = (f32[128,128]{1,0:T(8,128)}, f32[128,128]{1,0:T(8,128)}) custom-call(bf16[256,128]{1,0:T(8,128)(2,1)} %bitcast.4, bf16[128,128]{1,0:T(8,128)(2,1)} %bitcast.5, bf16[128,128]{1,0:T(8,128)(2,1)} %bitcast.6, bf16[2,128,1024]{2,1,0:T(8,128)(2,1)} %proj_hbm.1, bf16[128,128]{1,0:T(8,128)(2,1)} %signal_hbm.1, bf16[128,128]{1,0:T(8,128)(2,1)} %gate_hbm.1, ...), custom_call_target="tpu_custom_call" | custom-call | tf_op jit(solution)/shard_map/pallas_call | solution.py:489
  24.5 1.5 %copy.14 = f32[128,128]{1,0:T(8,128)} copy(f32[128,128]{1,0:T(8,128)} %get-tuple-element.4) | data formatting | bytes 131072
  26.0 1.5 %copy.15 = f32[128,128]{1,0:T(8,128)} copy(f32[128,128]{1,0:T(8,128)} %get-tuple-element.5) | data formatting | bytes 131072

commit v2 on v1

--- a/solution.py
+++ b/solution.py
@@ -344,74 +344,112 @@
     queries = jnp.dot(order, query_buf[...], preferred_element_type=jnp.float32).astype(jnp.bfloat16)
     pl.semaphore_wait(barrier, seq_n + group_n - 2)
 
-    def gather(kind, step, source, target):
+    gathered = (
+        lambda owner: key_buf.at[place(owner)],
+        lambda owner: value_buf.at[place(owner)],
+        lambda owner: pair_buf.at[signal_rows, place(owner)],
+        lambda owner: pair_buf.at[taps_rows, place(owner)],
+    )
+    sources = (key_hbm, value_hbm, signal_hbm, pair_buf.at[taps_rows, here])
+
+    def gather(kind, step, owner):
         return pltpu.make_async_remote_copy(
-            src_ref=source,
-            dst_ref=target,
+            src_ref=sources[kind],
+            dst_ref=gathered[kind](owner),
             send_sem=gather_send.at[kind, step],
-            recv_sem=gather_recv.at[kind, step],
+            recv_sem=gather_recv.at[kind, owner],
             device_id={"seq": seq_peer(step)},
             device_id_type=MESH,
         )
 
     far_first = sorted(range(1, seq_n), key=lambda step: abs(2 * step - seq_n))
     sends = []
-    for kind, source, target in (
-        (0, key_hbm, key_buf.at[here]),
-        (1, value_hbm, value_buf.at[here]),
-        (2, signal_hbm, pair_buf.at[signal_rows, here]),
-        (3, pair_buf.at[taps_rows, here], pair_buf.at[taps_rows, here]),
-    ):
+
+    def send_gather(kind):
         for step in far_first:
-            copy = gather(kind, step, source, target)
+            copy = gather(kind, step, mine)
             copy.start()
             sends.append(copy)
 
+    width = 2 if seq_n % 2 == 0 else 1
+
+    def chunk(step):
+        first = lax.rem(mine // width + step, seq_n // width) * width
+        if step:
+            owners = [first + inner for inner in range(width)]
+        else:
+            owners = [first + lax.rem(mine + 1, 2)] if width == 2 else []
+        return first, owners, pl.ds(pl.multiple_of(first * span, width * span), width * span)
+
+    send_gather(0)
+    send_gather(1)
     key_copy.wait()
     value_copy.wait()
-    for step in range(1, seq_n):
-        gather(0, step, key_hbm, key_buf.at[place(seq_from(step))]).wait_recv()
-    scores = dot_nt(queries, key_buf[...]) * (head_dim ** -0.5)
-    query_pos = mine * span + lax.broadcasted_iota(jnp.int32, scores.shape, 0) % span
-    key_pos = lax.broadcasted_iota(jnp.int32, scores.shape, 1)
-    live = key_pos <= query_pos
-    row_max = jnp.max(jnp.where(live, scores, -jnp.inf), axis=1, keepdims=True)
-    weight = jnp.where(live, jnp.exp(scores - row_max), 0.0)
-    row_sum = jnp.sum(weight, axis=1, keepdims=True)
-    for step in range(1, seq_n):
-        gather(1, step, value_hbm, value_buf.at[place(seq_from(step))]).wait_recv()
-    weighted = jnp.dot(weight.astype(jnp.bfloat16), value_buf[...], preferred_element_type=jnp.float32)
+    for step in range(seq_n // width):
+        first, owners, where = chunk(step)
+        for owner in owners:
+            gather(0, 1, owner).wait_recv()
+        scores = dot_nt(queries, key_buf[where, :]) * (head_dim ** -0.5)
+        query_pos = mine * span + lax.broadcasted_iota(jnp.int32, scores.shape, 0) % span
+        key_pos = first * span + lax.broadcasted_iota(jnp.int32, scores.shape, 1)
+        live = key_pos <= query_pos
+        scores = jnp.where(live, scores, -jnp.inf)
+        chunk_max = jnp.max(scores, axis=1, keepdims=True)
+        new_max = jnp.maximum(row_max, chunk_max) if step else chunk_max
+        weight = jnp.exp(scores - new_max)
+        chunk_sum = jnp.sum(weight, axis=1, keepdims=True)
+        for owner in owners:
+            gather(1, 1, owner).wait_recv()
+        if step == seq_n // width - 1:
+            send_gather(2)
+            send_gather(3)
+        product = jnp.dot(weight.astype(jnp.bfloat16), value_buf[where, :], preferred_element_type=jnp.float32)
+        if step:
+            rescale = jnp.exp(row_max - new_max)
+            row_sum = row_sum * rescale + chunk_sum
+            weighted = weighted * rescale + product
+        else:
+            row_sum, weighted = chunk_sum, product
+        row_max = new_max
     attended = (weighted / row_sum).astype(jnp.bfloat16)
 
     proj_copy.wait()
-    partial = jnp.dot(attended[:span], proj_buf[0], preferred_element_type=jnp.float32)
-    for head in range(1, heads):
-        partial = partial + jnp.dot(
-            attended[head * span:(head + 1) * span], proj_buf[head], preferred_element_type=jnp.float32
-        )
-    for block in range(group_n):
-        part_send[block] = partial[:, block * chans:(block + 1) * chans].astype(jnp.bfloat16)
-
-    def part_copy(step, slot):
-        other, device = group_peer(step)
+    def part_copy(other, slot):
         return pltpu.make_async_remote_copy(
             src_ref=part_send.at[other],
             dst_ref=part_recv.at[slot],
-            send_sem=part_send_sem.at[step],
-            recv_sem=part_recv_sem.at[step],
-            device_id=device,
+            send_sem=part_send_sem.at[other],
+            recv_sem=part_recv_sem.at[slot],
+            device_id={"role": other // head_n, "head": lax.rem(other, head_n)},
             device_id_type=MESH,
         )
 
-    for step in range(1, group_n):
-        copy = part_copy(step, step)
-        copy.start()
-        sends.append(copy)
+    couple = 2 if group_n % 2 == 0 else 1
+    for step in list(range(1, group_n // couple)) + [0]:
+        first = lax.rem(group // couple + step, group_n // couple) * couple
+        columns = pl.ds(pl.multiple_of(first * chans, couple * chans), couple * chans)
+        partial = 0.0
+        for head in range(heads):
+            partial = partial + jnp.dot(
+                attended[head * span:(head + 1) * span],
+                proj_buf[head, :, columns],
+                preferred_element_type=jnp.float32,
+            )
+        for inner in range(couple):
+            part_send[first + inner] = partial[:, inner * chans:(inner + 1) * chans].astype(jnp.bfloat16)
+        if step:
+            others = [first + inner for inner in range(couple)]
+        else:
+            others = [first + lax.rem(group + 1, 2)] if couple == 2 else []
+        for other in others:
+            copy = part_copy(other, group)
+            copy.start()
+            sends.append(copy)
 
     signal_copy.wait()
     for step in range(1, seq_n):
-        gather(2, step, signal_hbm, pair_buf.at[signal_rows, place(seq_from(step))]).wait_recv()
-        gather(3, step, pair_buf.at[taps_rows, here], pair_buf.at[taps_rows, place(seq_from(step))]).wait_recv()
+        gather(2, step, seq_from(step)).wait_recv()
+        gather(3, step, seq_from(step)).wait_recv()
     table_copy.wait()
     turned_copy.wait()
     gate_copy.wait()
@@ -430,8 +468,9 @@
 
     target = part_send[group].astype(jnp.float32)
     for step in range(1, group_n):
-        part_copy(step, step).wait_recv()
-        target = target + part_recv[step].astype(jnp.float32)
+        source = group_from(step)
+        part_copy(source, source).wait_recv()
+        target = target + part_recv[source].astype(jnp.float32)
     back = gate * (out_buf[...] - jnp.transpose(target))
     back_buf[:, here] = back.astype(jnp.bfloat16)
 
@@ -450,15 +489,11 @@
         copy = back_copy(step, mine)
         copy.start()
         sends.append(copy)
-    width = 2 if seq_n % 2 == 0 else 1
     back_spec = 0.0
     for step in range(seq_n // width):
-        first = lax.rem(mine // width + step, seq_n // width) * width
-        for owner in ([lax.rem(mine + 1, 2) + first] if step == 0 and width == 2 else []) + (
-            [first + inner for inner in range(width)] if step else []
-        ):
+        _, owners, where = chunk(step)
+        for owner in owners:
             back_copy(1, owner).wait_recv()
-        where = pl.ds(pl.multiple_of(first * span, width * span), width * span)
         back_spec = back_spec + forward(back_buf[:, where], table_buf, where)
     back_c, back_s = back_spec[:, :seq_total], back_spec[:, seq_total:]
 
@@ -471,6 +506,17 @@
     step_ref[...] = lags[chans:] * (seq_total ** -1.5)
     for copy in sends:
         copy.wait_send()
+
+
+def hand_over(grad_in, step_in, grad_out, step_out, sems):
+    copies = [
+        pltpu.make_async_copy(grad_in, grad_out, sems.at[0]),
+        pltpu.make_async_copy(step_in, step_out, sems.at[1]),
+    ]
+    for copy in copies:
+        copy.start()
+    for copy in copies:
+        copy.wait()
 
 
 def fused_body(query_heads, key_heads, value_heads, distill_proj, conv_input, gate_input, filter_taps, skip_gain):
@@ -486,7 +532,7 @@
     vmem = pl.BlockSpec(memory_space=pltpu.VMEM)
     bf16, f32 = jnp.bfloat16, jnp.float32
     dma = pltpu.SemaphoreType.DMA
-    return pl.pallas_call(
+    results = pl.pallas_call(
         functools.partial(fused_kernel, seq_n, role_n, head_n, heads),
         out_shape=[jax.ShapeDtypeStruct((chans, span), f32)] * 2,
         in_specs=[in_hbm] * 10,
@@ -530,6 +576,14 @@
         table,
         turned,
     )
+    return pl.pallas_call(
+        hand_over,
+        out_shape=[jax.ShapeDtypeStruct((chans, span), f32)] * 2,
+        in_specs=[in_hbm] * 2,
+        out_specs=[in_hbm] * 2,
+        scratch_shapes=[dma((2,))],
+        compiler_params=pltpu.CompilerParams(vmem_limit_bytes=63 * 1024 * 1024),
+    )(*results)
 
 
 def solution(mesh):

time: 27.7 us -> 28.6 us (1.032)
  Pallas kernels: 23.9 us -> 27.8 us
  local copies, waits for them, and re-layouts: 2.95 us -> 0 us
    pallas_call x0 -> x1, Pallas kernels: none -> 5.09 us  [fused_body(): pl.pallas_call(hand_over, out_shape=[jax.ShapeDtypeStruct((chans, span),...]
    unnamed x2 -> x0, local copies, waits for them, and re-layouts: 2.95 us -> none
    pallas_call x1, Pallas kernels: 23.9 us -> 22.7 us  [fused_body(): pl.pallas_call(functools.partial(fused_kernel, seq_n, role_n, head_n, hea...]
where the time goes in v2:
time: 28.6 us; the launch traced here: 28.4 us
  Pallas kernels  27.8 us (97%)
  between operations  0.64 us (2%)
    pallas_call x1, Pallas kernels, fused_body(): pl.pallas_call(functools.partial(fused_kernel, seq_n, role_n, head_n, hea...  22.7 us
    pallas_call x1, Pallas kernels, fused_body(): pl.pallas_call(hand_over, out_shape=[jax.ShapeDtypeStruct((chans, span),...  5.09 us

profile of v2, /device:TPU:0, one launch (start us, length us, event | category | flops | bytes accessed | tf_op | source)
XLA Modules:
  0.0 28.4 jit_solution(2882209192405476670)
XLA Ops:
  0.6 22.7 %shard_map.113 = (f32[128,128]{1,0:T(8,128)}, f32[128,128]{1,0:T(8,128)}) custom-call(bf16[256,128]{1,0:T(8,128)(2,1)} %bitcast.4, bf16[128,128]{1,0:T(8,128)(2,1)} %bitcast.5, bf16[128,128]{1,0:T(8,128)(2,1)} %bitcast.6, bf16[2,128,1024]{2,1,0:T(8,128)(2,1)} %proj_hbm.1, bf16[128,128]{1,0:T(8,128)(2,1)} %signal_hbm.1, bf16[128,128]{1,0:T(8,128)(2,1)} %gate_hbm.1, ...), custom_call_target="tpu_custom_call" | custom-call | tf_op jit(solution)/shard_map/pallas_call | solution.py:535
  23.3 5.1 %shard_map.114 = (f32[128,128]{1,0:T(8,128)}, f32[128,128]{1,0:T(8,128)}) custom-call(f32[128,128]{1,0:T(8,128)} %get-tuple-element.4.grad_in, f32[128,128]{1,0:T(8,128)} %get-tuple-element.5.step_in), custom_call_target="tpu_custom_call" | custom-call | tf_op jit(solution)/shard_map/pallas_call | solution.py:579

commit v3 on v2

--- a/solution.py
+++ b/solution.py
@@ -269,10 +269,10 @@
 def inverse(spec, turned_buf):
     upper = spec.astype(jnp.bfloat16)
     lower = (spec - upper.astype(jnp.float32)).astype(jnp.bfloat16)
-    both = jnp.concatenate([upper, lower], axis=0)
-    first = jnp.dot(both, turned_buf[0], preferred_element_type=jnp.float32)
-    second = jnp.dot(upper, turned_buf[1], preferred_element_type=jnp.float32)
-    return first[: spec.shape[0]] + (first[spec.shape[0]:] + second)
+    width = turned_buf.shape[1] // 2
+    wide = jnp.dot(upper, turned_buf[...], preferred_element_type=jnp.float32)
+    rest = jnp.dot(lower, turned_buf[:, :width], preferred_element_type=jnp.float32)
+    return wide[:, :width] + (wide[:, width:] + rest)
 
 
 def fused_kernel(
@@ -321,7 +321,7 @@
             (gate_hbm, gate_buf),
             (skip_hbm, skip_buf),
             (table_hbm, table_buf),
-            (turned_hbm.at[:, :, here], turned_buf),
+            (turned_hbm.at[:, pl.ds(pl.multiple_of(2 * mine * span, 2 * span), 2 * span)], turned_buf),
         ])
     ]
     for copy in locals_:
@@ -425,7 +425,7 @@
         )
 
     couple = 2 if group_n % 2 == 0 else 1
-    for step in list(range(1, group_n // couple)) + [0]:
+    for step in list(range(1, group_n // couple, 2)) + list(range(2, group_n // couple, 2)) + [0]:
         first = lax.rem(group // couple + step, group_n // couple) * couple
         columns = pl.ds(pl.multiple_of(first * chans, couple * chans), couple * chans)
         partial = 0.0
@@ -508,14 +508,21 @@
         copy.wait_send()
 
 
-def hand_over(grad_in, step_in, grad_out, step_out, sems):
-    copies = [
-        pltpu.make_async_copy(grad_in, grad_out, sems.at[0]),
-        pltpu.make_async_copy(step_in, step_out, sems.at[1]),
+def hand_over(grad_in, step_in, grad_out, step_out, held, sems):
+    arriving = [
+        pltpu.make_async_copy(source, held.at[index], sems.at[index])
+        for index, source in enumerate((grad_in, step_in))
     ]
-    for copy in copies:
+    leaving = [
+        pltpu.make_async_copy(held.at[index], target, sems.at[2 + index])
+        for index, target in enumerate((grad_out, step_out))
+    ]
+    for copy in arriving:
         copy.start()
-    for copy in copies:
+    for first, second in zip(arriving, leaving):
+        first.wait()
+        second.start()
+    for copy in leaving:
         copy.wait()
 
 
@@ -527,7 +534,8 @@
     chans = conv_input.shape[0]
     table_terms = half_step_table(seq_total)
     table = jnp.asarray(table_terms)
-    turned = jnp.asarray(np.ascontiguousarray(np.swapaxes(table_terms, 1, 2)))
+    turned = table_terms.reshape(2, seq_n, span, 2 * seq_total).transpose(3, 1, 0, 2)
+    turned = jnp.asarray(np.ascontiguousarray(turned.reshape(2 * seq_total, 2 * seq_total)))
     in_hbm = pl.BlockSpec(memory_space=pltpu.HBM)
     vmem = pl.BlockSpec(memory_space=pltpu.VMEM)
     bf16, f32 = jnp.bfloat16, jnp.float32
@@ -546,7 +554,7 @@
             pltpu.VMEM((chans, span), f32),
             pltpu.VMEM((1, chans), f32),
             pltpu.VMEM(table.shape, bf16),
-            pltpu.VMEM((2, 2 * seq_total, span), bf16),
+            pltpu.VMEM((2 * seq_total, 2 * span), bf16),
             pltpu.VMEM((2 * chans, seq_total), bf16),
             pltpu.VMEM((2 * chans, 2 * seq_total), f32),
             pltpu.VMEM((chans, span), f32),
@@ -581,7 +589,7 @@
         out_shape=[jax.ShapeDtypeStruct((chans, span), f32)] * 2,
         in_specs=[in_hbm] * 2,
         out_specs=[in_hbm] * 2,
-        scratch_shapes=[dma((2,))],
+        scratch_shapes=[pltpu.VMEM((2, chans, span), f32), dma((4,))],
         compiler_params=pltpu.CompilerParams(vmem_limit_bytes=63 * 1024 * 1024),
     )(*results)
 

time: 28.6 us -> 24.9 us (0.87)
  Pallas kernels: 27.8 us -> 24.1 us
    pallas_call x1, Pallas kernels: 5.09 us -> 1.53 us  [fused_body(): pl.pallas_call(hand_over, out_shape=[jax.ShapeDtypeStruct((chans, span),...]
where the time goes in v3:
time: 24.9 us; the launch traced here: 24.7 us
  Pallas kernels  24.1 us (97%)
  between operations  0.64 us (3%)
    pallas_call x1, Pallas kernels, fused_body(): pl.pallas_call(functools.partial(fused_kernel, seq_n, role_n, head_n, hea...  22.5 us
    pallas_call x1, Pallas kernels, fused_body(): pl.pallas_call(hand_over, out_shape=[jax.ShapeDtypeStruct((chans, span),...  1.53 us

profile of v3, /device:TPU:0, one launch (start us, length us, event | category | flops | bytes accessed | tf_op | source)
XLA Modules:
  0.0 24.7 jit_solution(15488095592268920516)
XLA Ops:
  0.6 22.5 %shard_map.113 = (f32[128,128]{1,0:T(8,128)}, f32[128,128]{1,0:T(8,128)}) custom-call(bf16[256,128]{1,0:T(8,128)(2,1)} %bitcast.4, bf16[128,128]{1,0:T(8,128)(2,1)} %bitcast.5, bf16[128,128]{1,0:T(8,128)(2,1)} %bitcast.6, bf16[2,128,1024]{2,1,0:T(8,128)(2,1)} %proj_hbm.1, bf16[128,128]{1,0:T(8,128)(2,1)} %signal_hbm.1, bf16[128,128]{1,0:T(8,128)(2,1)} %gate_hbm.1, ...), custom_call_target="tpu_custom_call" | custom-call | tf_op jit(solution)/shard_map/pallas_call | solution.py:543
  23.2 1.5 %shard_map.114 = (f32[128,128]{1,0:T(8,128)}, f32[128,128]{1,0:T(8,128)}) custom-call(f32[128,128]{1,0:T(8,128)} %get-tuple-element.4.grad_in, f32[128,128]{1,0:T(8,128)} %get-tuple-element.5.step_in), custom_call_target="tpu_custom_call" | custom-call | tf_op jit(solution)/shard_map/pallas_call | solution.py:587

commit v4 on v2

--- a/solution.py
+++ b/solution.py
@@ -269,10 +269,10 @@
 def inverse(spec, turned_buf):
     upper = spec.astype(jnp.bfloat16)
     lower = (spec - upper.astype(jnp.float32)).astype(jnp.bfloat16)
-    both = jnp.concatenate([upper, lower], axis=0)
-    first = jnp.dot(both, turned_buf[0], preferred_element_type=jnp.float32)
-    second = jnp.dot(upper, turned_buf[1], preferred_element_type=jnp.float32)
-    return first[: spec.shape[0]] + (first[spec.shape[0]:] + second)
+    width = turned_buf.shape[1] // 2
+    wide = jnp.dot(upper, turned_buf[...], preferred_element_type=jnp.float32)
+    rest = jnp.dot(lower, turned_buf[:, :width], preferred_element_type=jnp.float32)
+    return wide[:, :width] + (wide[:, width:] + rest)
 
 
 def fused_kernel(
@@ -321,7 +321,7 @@
             (gate_hbm, gate_buf),
             (skip_hbm, skip_buf),
             (table_hbm, table_buf),
-            (turned_hbm.at[:, :, here], turned_buf),
+            (turned_hbm.at[:, pl.ds(pl.multiple_of(2 * mine * span, 2 * span), 2 * span)], turned_buf),
         ])
     ]
     for copy in locals_:
@@ -425,7 +425,7 @@
         )
 
     couple = 2 if group_n % 2 == 0 else 1
-    for step in list(range(1, group_n // couple)) + [0]:
+    for step in list(range(1, group_n // couple, 2)) + list(range(2, group_n // couple, 2)) + [0]:
         first = lax.rem(group // couple + step, group_n // couple) * couple
         columns = pl.ds(pl.multiple_of(first * chans, couple * chans), couple * chans)
         partial = 0.0
@@ -527,14 +527,27 @@
     chans = conv_input.shape[0]
     table_terms = half_step_table(seq_total)
     table = jnp.asarray(table_terms)
-    turned = jnp.asarray(np.ascontiguousarray(np.swapaxes(table_terms, 1, 2)))
+    turned = table_terms.reshape(2, seq_n, span, 2 * seq_total).transpose(3, 1, 0, 2)
+    turned = jnp.asarray(np.ascontiguousarray(turned.reshape(2 * seq_total, 2 * seq_total)))
     in_hbm = pl.BlockSpec(memory_space=pltpu.HBM)
     vmem = pl.BlockSpec(memory_space=pltpu.VMEM)
     bf16, f32 = jnp.bfloat16, jnp.float32
     dma = pltpu.SemaphoreType.DMA
+    operands = (
+        query_heads.reshape(span * heads, head_dim),
+        key_heads.reshape(span, head_dim),
+        value_heads.reshape(span, head_dim),
+        distill_proj,
+        conv_input,
+        gate_input,
+        filter_taps,
+        skip_gain.reshape(1, chans),
+        table,
+        turned,
+    )
     results = pl.pallas_call(
         functools.partial(fused_kernel, seq_n, role_n, head_n, heads),
-        out_shape=[jax.ShapeDtypeStruct((chans, span), f32)] * 2,
+        out_shape=[pltpu.VMEM((chans, span), f32)] * 2,
         in_specs=[in_hbm] * 10,
         out_specs=[vmem, vmem],
         scratch_shapes=[
@@ -546,7 +559,7 @@
             pltpu.VMEM((chans, span), f32),
             pltpu.VMEM((1, chans), f32),
             pltpu.VMEM(table.shape, bf16),
-            pltpu.VMEM((2, 2 * seq_total, span), bf16),
+            pltpu.VMEM((2 * seq_total, 2 * span), bf16),
             pltpu.VMEM((2 * chans, seq_total), bf16),
             pltpu.VMEM((2 * chans, 2 * seq_total), f32),
             pltpu.VMEM((chans, span), f32),
@@ -562,27 +575,16 @@
             dma((seq_n,)),
         ],
         compiler_params=pltpu.CompilerParams(
-            collective_id=0, has_side_effects=True, vmem_limit_bytes=63 * 1024 * 1024
+            collective_id=0, has_side_effects=True, vmem_limit_bytes=40 * 1024 * 1024
         ),
-    )(
-        query_heads.reshape(span * heads, head_dim),
-        key_heads.reshape(span, head_dim),
-        value_heads.reshape(span, head_dim),
-        distill_proj,
-        conv_input,
-        gate_input,
-        filter_taps,
-        skip_gain.reshape(1, chans),
-        table,
-        turned,
-    )
+    )(*[pltpu.with_memory_space_constraint(operand, pltpu.HBM) for operand in operands])
     return pl.pallas_call(
         hand_over,
         out_shape=[jax.ShapeDtypeStruct((chans, span), f32)] * 2,
-        in_specs=[in_hbm] * 2,
+        in_specs=[pl.BlockSpec(memory_space=pl.ANY)] * 2,
         out_specs=[in_hbm] * 2,
         scratch_shapes=[dma((2,))],
-        compiler_params=pltpu.CompilerParams(vmem_limit_bytes=63 * 1024 * 1024),
+        compiler_params=pltpu.CompilerParams(vmem_limit_bytes=40 * 1024 * 1024),
     )(*results)
 
 

time: 28.6 us -> 23.3 us (0.81)
  Pallas kernels: 27.8 us -> 22.5 us
    pallas_call x1, Pallas kernels: 5.09 us -> 0.67 us  [fused_body(): pl.pallas_call(hand_over, out_shape=[jax.ShapeDtypeStruct((chans, span),...]
    pallas_call x1, Pallas kernels: 22.7 us -> 21.9 us  [fused_body(): pl.pallas_call(functools.partial(fused_kernel, seq_n, role_n, head_n, hea...]
where the time goes in v4:
time: 23.3 us; the launch traced here: 23.2 us
  Pallas kernels  22.5 us (97%)
  between operations  0.64 us (3%)
    pallas_call x1, Pallas kernels, fused_body(): pl.pallas_call(functools.partial(fused_kernel, seq_n, role_n, head_n, hea...  21.9 us
    pallas_call x1, Pallas kernels, fused_body(): pl.pallas_call(hand_over, out_shape=[jax.ShapeDtypeStruct((chans, span),...  0.67 us

profile of v4, /device:TPU:0, one launch (start us, length us, event | category | flops | bytes accessed | tf_op | source)
XLA Modules:
  0.0 23.2 jit_solution(13331217154353497945)
XLA Ops:
  0.6 21.9 %shard_map.113 = (f32[128,128]{1,0:T(8,128)S(1)}, f32[128,128]{1,0:T(8,128)S(1)}) custom-call(bf16[256,128]{1,0:T(8,128)(2,1)} %bitcast.4, bf16[128,128]{1,0:T(8,128)(2,1)} %bitcast.5, bf16[128,128]{1,0:T(8,128)(2,1)} %bitcast.6, bf16[2,128,1024]{2,1,0:T(8,128)(2,1)} %proj_hbm.1, bf16[128,128]{1,0:T(8,128)(2,1)} %signal_hbm.1, bf16[128,128]{1,0:T(8,128)(2,1)} %gate_hbm.1, ...), custom_call_target="tpu_custom_call" | custom-call | tf_op jit(solution)/shard_map/pallas_call | solution.py:548
  22.5 0.7 %shard_map.114 = (f32[128,128]{1,0:T(8,128)}, f32[128,128]{1,0:T(8,128)}) custom-call(f32[128,128]{1,0:T(8,128)S(1)} %get-tuple-element.4.grad_in, f32[128,128]{1,0:T(8,128)S(1)} %get-tuple-element.5.step_in), custom_call_target="tpu_custom_call" | custom-call | tf_op jit(solution)/shard_map/pallas_call | solution.py:581

commit v5 on v4

--- a/solution.py
+++ b/solution.py
@@ -335,10 +335,12 @@
         pl.semaphore_signal(barrier, inc=1, device_id=group_peer(step)[1], device_id_type=MESH)
     taps_copy.wait()
     pair_buf[taps_rows, here] = taps_buf[...].astype(jnp.bfloat16)
+    half_span = span // 2
+    part_rows = heads * half_span
     rows = query_buf.shape[0]
     row_id = lax.broadcasted_iota(jnp.int32, (rows, rows), 0)
     col_id = lax.broadcasted_iota(jnp.int32, (rows, rows), 1)
-    wanted = (row_id % span) * heads + row_id // span
+    wanted = (row_id // part_rows * half_span + row_id % half_span) * heads + row_id % part_rows // half_span
     order = jnp.where(col_id == wanted, 1.0, 0.0).astype(jnp.bfloat16)
     query_copy.wait()
     queries = jnp.dot(order, query_buf[...], preferred_element_type=jnp.float32).astype(jnp.bfloat16)
@@ -385,66 +387,74 @@
     send_gather(1)
     key_copy.wait()
     value_copy.wait()
-    for step in range(seq_n // width):
-        first, owners, where = chunk(step)
-        for owner in owners:
+    chunks = seq_n // width
+
+    def attend(step, begin, end, state):
+        first, _, where = chunk(step)
+        scores = dot_nt(queries[begin:end], key_buf[where, :]) * (head_dim ** -0.5)
+        row = begin + lax.broadcasted_iota(jnp.int32, scores.shape, 0)
+        query_pos = mine * span + row // part_rows * half_span + row % half_span
+        key_pos = first * span + lax.broadcasted_iota(jnp.int32, scores.shape, 1)
+        scores = jnp.where(key_pos <= query_pos, scores, -jnp.inf)
+        new_max = jnp.max(scores, axis=1, keepdims=True)
+        if state is not None:
+            new_max = jnp.maximum(new_max, state[0][begin:end])
+        weight = jnp.exp(scores - new_max)
+        row_sum = jnp.sum(weight, axis=1, keepdims=True)
+        weighted = jnp.dot(weight.astype(jnp.bfloat16), value_buf[where, :], preferred_element_type=jnp.float32)
+        if state is not None:
+            rescale = jnp.exp(state[0][begin:end] - new_max)
+            row_sum = row_sum + state[1][begin:end] * rescale
+            weighted = weighted + state[2][begin:end] * rescale
+        return new_max, row_sum, weighted
+
+    state = None
+    for step in range(chunks):
+        for owner in chunk(step)[1]:
             gather(0, 1, owner).wait_recv()
-        scores = dot_nt(queries, key_buf[where, :]) * (head_dim ** -0.5)
-        query_pos = mine * span + lax.broadcasted_iota(jnp.int32, scores.shape, 0) % span
-        key_pos = first * span + lax.broadcasted_iota(jnp.int32, scores.shape, 1)
-        live = key_pos <= query_pos
-        scores = jnp.where(live, scores, -jnp.inf)
-        chunk_max = jnp.max(scores, axis=1, keepdims=True)
-        new_max = jnp.maximum(row_max, chunk_max) if step else chunk_max
-        weight = jnp.exp(scores - new_max)
-        chunk_sum = jnp.sum(weight, axis=1, keepdims=True)
-        for owner in owners:
             gather(1, 1, owner).wait_recv()
-        if step == seq_n // width - 1:
-            send_gather(2)
-            send_gather(3)
-        product = jnp.dot(weight.astype(jnp.bfloat16), value_buf[where, :], preferred_element_type=jnp.float32)
-        if step:
-            rescale = jnp.exp(row_max - new_max)
-            row_sum = row_sum * rescale + chunk_sum
-            weighted = weighted * rescale + product
-        else:
-            row_sum, weighted = chunk_sum, product
-        row_max = new_max
-    attended = (weighted / row_sum).astype(jnp.bfloat16)
-
+        if step < chunks - 1:
+            state = attend(step, 0, rows, state)
+    send_gather(2)
+    send_gather(3)
     proj_copy.wait()
-    def part_copy(other, slot):
+
+    def part_copy(other, slot, half):
+        piece = pl.ds(half * half_span, half_span)
         return pltpu.make_async_remote_copy(
-            src_ref=part_send.at[other],
-            dst_ref=part_recv.at[slot],
-            send_sem=part_send_sem.at[other],
-            recv_sem=part_recv_sem.at[slot],
+            src_ref=part_send.at[other, piece],
+            dst_ref=part_recv.at[slot, piece],
+            send_sem=part_send_sem.at[other, half],
+            recv_sem=part_recv_sem.at[slot, half],
             device_id={"role": other // head_n, "head": lax.rem(other, head_n)},
             device_id_type=MESH,
         )
 
     couple = 2 if group_n % 2 == 0 else 1
-    for step in list(range(1, group_n // couple, 2)) + list(range(2, group_n // couple, 2)) + [0]:
-        first = lax.rem(group // couple + step, group_n // couple) * couple
-        columns = pl.ds(pl.multiple_of(first * chans, couple * chans), couple * chans)
-        partial = 0.0
-        for head in range(heads):
-            partial = partial + jnp.dot(
-                attended[head * span:(head + 1) * span],
-                proj_buf[head, :, columns],
-                preferred_element_type=jnp.float32,
-            )
-        for inner in range(couple):
-            part_send[first + inner] = partial[:, inner * chans:(inner + 1) * chans].astype(jnp.bfloat16)
-        if step:
-            others = [first + inner for inner in range(couple)]
-        else:
-            others = [first + lax.rem(group + 1, 2)] if couple == 2 else []
-        for other in others:
-            copy = part_copy(other, group)
-            copy.start()
-            sends.append(copy)
+    couples = group_n // couple
+    for half in range(2):
+        begin = half * part_rows
+        _, row_sum, weighted = attend(chunks - 1, begin, begin + part_rows, state)
+        attended = (weighted / row_sum).astype(jnp.bfloat16)
+        attended = jnp.concatenate(
+            [attended[head * half_span:(head + 1) * half_span] for head in range(heads)], axis=1
+        )
+        for step in list(range(1, couples, 2)) + list(range(2, couples, 2)) + [0]:
+            first = lax.rem(group // couple + step, couples) * couple
+            columns = pl.ds(pl.multiple_of(first * chans, couple * chans), couple * chans)
+            partial = jnp.dot(attended, proj_buf[:, columns], preferred_element_type=jnp.float32)
+            for inner in range(couple):
+                part_send[first + inner, pl.ds(half * half_span, half_span)] = partial[
+                    :, inner * chans:(inner + 1) * chans
+                ].astype(jnp.bfloat16)
+            if step:
+                others = [first + inner for inner in range(couple)]
+            else:
+                others = [first + lax.rem(group + 1, 2)] if couple == 2 else []
+            for other in others:
+                copy = part_copy(other, group, half)
+                copy.start()
+                sends.append(copy)
 
     signal_copy.wait()
     for step in range(1, seq_n):
@@ -469,7 +479,8 @@
     target = part_send[group].astype(jnp.float32)
     for step in range(1, group_n):
         source = group_from(step)
-        part_copy(source, source).wait_recv()
+        part_copy(source, source, 0).wait_recv()
+        part_copy(source, source, 1).wait_recv()
         target = target + part_recv[source].astype(jnp.float32)
     back = gate * (out_buf[...] - jnp.transpose(target))
     back_buf[:, here] = back.astype(jnp.bfloat16)
@@ -537,7 +548,7 @@
         query_heads.reshape(span * heads, head_dim),
         key_heads.reshape(span, head_dim),
         value_heads.reshape(span, head_dim),
-        distill_proj,
+        distill_proj.reshape(heads * head_dim, distill_proj.shape[2]),
         conv_input,
         gate_input,
         filter_taps,
@@ -554,7 +565,7 @@
             pltpu.VMEM((span * heads, head_dim), bf16),
             pltpu.VMEM((seq_total, head_dim), bf16),
             pltpu.VMEM((seq_total, head_dim), bf16),
-            pltpu.VMEM(distill_proj.shape, bf16),
+            pltpu.VMEM((heads * head_dim, distill_proj.shape[2]), bf16),
             pltpu.VMEM((chans, span), bf16),
             pltpu.VMEM((chans, span), f32),
             pltpu.VMEM((1, chans), f32),
@@ -569,8 +580,8 @@
             dma((10,)),
             dma((4, seq_n)),
             dma((4, seq_n)),
-            dma((group_n,)),
-            dma((group_n,)),
+            dma((group_n, 2)),
+            dma((group_n, 2)),
             dma((seq_n,)),
             dma((seq_n,)),
         ],

time: 23.3 us -> 23.8 us (1.021)
  Pallas kernels: 22.5 us -> 23 us
    pallas_call x1, Pallas kernels: 21.9 us -> 22.3 us  [fused_body(): pl.pallas_call(functools.partial(fused_kernel, seq_n, role_n, head_n, hea...]
where the time goes in v5:
time: 23.8 us; the launch traced here: 23.6 us
  Pallas kernels  23 us (97%)
  between operations  0.64 us (3%)
    pallas_call x1, Pallas kernels, fused_body(): pl.pallas_call(functools.partial(fused_kernel, seq_n, role_n, head_n, hea...  22.3 us
    pallas_call x1, Pallas kernels, fused_body(): pl.pallas_call(hand_over, out_shape=[jax.ShapeDtypeStruct((chans, span),...  0.67 us

profile of v5, /device:TPU:0, one launch (start us, length us, event | category | flops | bytes accessed | tf_op | source)
XLA Modules:
  0.0 23.6 jit_solution(2095445544162806449)
XLA Ops:
  0.6 22.3 %shard_map.113 = (f32[128,128]{1,0:T(8,128)S(1)}, f32[128,128]{1,0:T(8,128)S(1)}) custom-call(bf16[256,128]{1,0:T(8,128)(2,1)} %bitcast.6, bf16[128,128]{1,0:T(8,128)(2,1)} %bitcast.7, bf16[128,128]{1,0:T(8,128)(2,1)} %bitcast.8, bf16[256,1024]{1,0:T(8,128)(2,1)} %bitcast.5, bf16[128,128]{1,0:T(8,128)(2,1)} %signal_hbm.1, bf16[128,128]{1,0:T(8,128)(2,1)} %gate_hbm.1, ...), custom_call_target="tpu_custom_call" | custom-call | tf_op jit(solution)/shard_map/pallas_call | solution.py:559
  22.9 0.7 %shard_map.114 = (f32[128,128]{1,0:T(8,128)}, f32[128,128]{1,0:T(8,128)}) custom-call(f32[128,128]{1,0:T(8,128)S(1)} %get-tuple-element.4.grad_in, f32[128,128]{1,0:T(8,128)S(1)} %get-tuple-element.5.step_in), custom_call_target="tpu_custom_call" | custom-call | tf_op jit(solution)/shard_map/pallas_call | solution.py:592

commit v6 on v4

--- a/solution.py
+++ b/solution.py
@@ -352,24 +352,18 @@
     )
     sources = (key_hbm, value_hbm, signal_hbm, pair_buf.at[taps_rows, here])
 
-    def gather(kind, step, owner):
+    def gather(kind, index, owner, peer):
         return pltpu.make_async_remote_copy(
             src_ref=sources[kind],
             dst_ref=gathered[kind](owner),
-            send_sem=gather_send.at[kind, step],
+            send_sem=gather_send.at[kind, index],
             recv_sem=gather_recv.at[kind, owner],
-            device_id={"seq": seq_peer(step)},
+            device_id={"seq": peer},
             device_id_type=MESH,
         )
 
     far_first = sorted(range(1, seq_n), key=lambda step: abs(2 * step - seq_n))
     sends = []
-
-    def send_gather(kind):
-        for step in far_first:
-            copy = gather(kind, step, mine)
-            copy.start()
-            sends.append(copy)
 
     width = 2 if seq_n % 2 == 0 else 1
 
@@ -381,14 +375,25 @@
             owners = [first + lax.rem(mine + 1, 2)] if width == 2 else []
         return first, owners, pl.ds(pl.multiple_of(first * span, width * span), width * span)
 
-    send_gather(0)
-    send_gather(1)
+    def send_gather(kind, steps):
+        for step in steps:
+            for inner, peer in enumerate(chunk(step)[1]):
+                copy = gather(kind, step * width + inner, mine, peer)
+                copy.start()
+                sends.append(copy)
+
+    chunks = seq_n // width
+    later = list(range(1, chunks))
+    for kind in (0, 1):
+        send_gather(kind, later + [0])
+    for kind in (2, 3):
+        send_gather(kind, [0])
     key_copy.wait()
     value_copy.wait()
     for step in range(seq_n // width):
         first, owners, where = chunk(step)
         for owner in owners:
-            gather(0, 1, owner).wait_recv()
+            gather(0, 0, owner, owner).wait_recv()
         scores = dot_nt(queries, key_buf[where, :]) * (head_dim ** -0.5)
         query_pos = mine * span + lax.broadcasted_iota(jnp.int32, scores.shape, 0) % span
         key_pos = first * span + lax.broadcasted_iota(jnp.int32, scores.shape, 1)
@@ -399,10 +404,10 @@
         weight = jnp.exp(scores - new_max)
         chunk_sum = jnp.sum(weight, axis=1, keepdims=True)
         for owner in owners:
-            gather(1, 1, owner).wait_recv()
-        if step == seq_n // width - 1:
-            send_gather(2)
-            send_gather(3)
+            gather(1, 0, owner, owner).wait_recv()
+        if step == chunks - 1:
+            for kind in (2, 3):
+                send_gather(kind, later)
         product = jnp.dot(weight.astype(jnp.bfloat16), value_buf[where, :], preferred_element_type=jnp.float32)
         if step:
             rescale = jnp.exp(row_max - new_max)
@@ -411,8 +416,16 @@
         else:
             row_sum, weighted = chunk_sum, product
         row_max = new_max
+        if step == 0:
+            signal_copy.wait()
+            table_copy.wait()
+            for owner in owners:
+                gather(2, 0, owner, owner).wait_recv()
+                gather(3, 0, owner, owner).wait_recv()
+            spec_buf[...] = forward(pair_buf[:, where], table_buf, where)
     attended = (weighted / row_sum).astype(jnp.bfloat16)
 
+    attended = jnp.concatenate([attended[head * span:(head + 1) * span] for head in range(heads)], axis=1)
     proj_copy.wait()
     def part_copy(other, slot):
         return pltpu.make_async_remote_copy(
@@ -428,13 +441,7 @@
     for step in list(range(1, group_n // couple, 2)) + list(range(2, group_n // couple, 2)) + [0]:
         first = lax.rem(group // couple + step, group_n // couple) * couple
         columns = pl.ds(pl.multiple_of(first * chans, couple * chans), couple * chans)
-        partial = 0.0
-        for head in range(heads):
-            partial = partial + jnp.dot(
-                attended[head * span:(head + 1) * span],
-                proj_buf[head, :, columns],
-                preferred_element_type=jnp.float32,
-            )
+        partial = jnp.dot(attended, proj_buf[:, columns], preferred_element_type=jnp.float32)
         for inner in range(couple):
             part_send[first + inner] = partial[:, inner * chans:(inner + 1) * chans].astype(jnp.bfloat16)
         if step:
@@ -446,15 +453,15 @@
             copy.start()
             sends.append(copy)
 
-    signal_copy.wait()
-    for step in range(1, seq_n):
-        gather(2, step, seq_from(step)).wait_recv()
-        gather(3, step, seq_from(step)).wait_recv()
-    table_copy.wait()
     turned_copy.wait()
     gate_copy.wait()
     skip_copy.wait()
-    spec_buf[...] = forward(pair_buf[...], table_buf, slice(None))
+    for step in later:
+        _, owners, where = chunk(step)
+        for owner in owners:
+            gather(2, 0, owner, owner).wait_recv()
+            gather(3, 0, owner, owner).wait_recv()
+        spec_buf[...] += forward(pair_buf[:, where], table_buf, where)
     low, high = pl.ds(0, seq_total), pl.ds(seq_total, seq_total)
     input_c, input_s = spec_buf[signal_rows, low], spec_buf[signal_rows, high]
     taps_c, taps_s = spec_buf[taps_rows, low], spec_buf[taps_rows, high]
@@ -537,7 +544,7 @@
         query_heads.reshape(span * heads, head_dim),
         key_heads.reshape(span, head_dim),
         value_heads.reshape(span, head_dim),
-        distill_proj,
+        distill_proj.reshape(heads * head_dim, distill_proj.shape[2]),
         conv_input,
         gate_input,
         filter_taps,
@@ -554,7 +561,7 @@
             pltpu.VMEM((span * heads, head_dim), bf16),
             pltpu.VMEM((seq_total, head_dim), bf16),
             pltpu.VMEM((seq_total, head_dim), bf16),
-            pltpu.VMEM(distill_proj.shape, bf16),
+            pltpu.VMEM((heads * head_dim, distill_proj.shape[2]), bf16),
             pltpu.VMEM((chans, span), bf16),
             pltpu.VMEM((chans, span), f32),
             pltpu.VMEM((1, chans), f32),

time: 23.3 us -> 23.3 us (level)
  no operation moved by 1% of the time
where the time goes in v6:
time: 23.3 us; the launch traced here: 23.2 us
  Pallas kernels  22.5 us (97%)
  between operations  0.64 us (3%)
    pallas_call x1, Pallas kernels, fused_body(): pl.pallas_call(functools.partial(fused_kernel, seq_n, role_n, head_n, hea...  21.8 us
    pallas_call x1, Pallas kernels, fused_body(): pl.pallas_call(hand_over, out_shape=[jax.ShapeDtypeStruct((chans, span),...  0.67 us

profile of v6, /device:TPU:0, one launch (start us, length us, event | category | flops | bytes accessed | tf_op | source)
XLA Modules:
  0.0 23.2 jit_solution(18075359476965206531)
XLA Ops:
  0.6 21.8 %shard_map.113 = (f32[128,128]{1,0:T(8,128)S(1)}, f32[128,128]{1,0:T(8,128)S(1)}) custom-call(bf16[256,128]{1,0:T(8,128)(2,1)} %bitcast.6, bf16[128,128]{1,0:T(8,128)(2,1)} %bitcast.7, bf16[128,128]{1,0:T(8,128)(2,1)} %bitcast.8, bf16[256,1024]{1,0:T(8,128)(2,1)} %bitcast.5, bf16[128,128]{1,0:T(8,128)(2,1)} %signal_hbm.1, bf16[128,128]{1,0:T(8,128)(2,1)} %gate_hbm.1, ...), custom_call_target="tpu_custom_call" | custom-call | tf_op jit(solution)/shard_map/pallas_call | solution.py:555
  22.5 0.7 %shard_map.114 = (f32[128,128]{1,0:T(8,128)}, f32[128,128]{1,0:T(8,128)}) custom-call(f32[128,128]{1,0:T(8,128)S(1)} %get-tuple-element.4.grad_in, f32[128,128]{1,0:T(8,128)S(1)} %get-tuple-element.5.step_in), custom_call_target="tpu_custom_call" | custom-call | tf_op jit(solution)/shard_map/pallas_call | solution.py:588
